TPU v7x, 1024 devices: a whole 8x8x8 slice. The times are simulated.
1024 devices in a mesh: dp: 16 (over y, core), expert: 64 (over x, z).
Axes of the slice: x: 8, y: 8, z: 8, core: 2. Of those that a mesh axis runs over, the one named last changes fastest.
Arguments:
- grad_out: bfloat16 [131072, 2048], P(('dp', 'expert')), may hold values from -6 to 6
- route_ids: int32 [131072, 2], P(('dp', 'expert')), may hold values from 0 to 127, all different within a row; in each aligned block of 128 rows (0 to 127, 128 to 255, ...) at most 4 rows name the same one
- route_probs: float32 [131072, 2], P(('dp', 'expert')), may hold values from 0.01 to 0.3
- hidden: bfloat16 [16, 64, 128, 4, 768], P('dp', None, 'expert'), may hold values from -2 to 2
- w_down: bfloat16 [128, 768, 2048], P('expert'), may hold values from -0.21875 to 0.21875
Outputs:
- hidden_grad: bfloat16 [16, 64, 128, 4, 768], P('dp', None, 'expert')
- prob_grad: float32 [131072, 2], P(('dp', 'expert'))
- weight_grad: float32 [768, 128, 2048], P('dp', 'expert')
Inputs may be any that keep to these rules, and one draw needn't show every extreme that they name: `route_ids`: each row names 2 different experts; among the 128 rows of one device no expert is named more than 4 times, a bound that some block reaches.
All inputs are finite; a program needn't handle non-finite values.
Results may differ from a plain program's by a relative error of at most 0.022.
Values may be sent and summed in bfloat16 or wider, within the bound.
A program may use at most 128 MiB of HBM per device.

v0:
```python
import jax
import jax.numpy as jnp
from jax import lax
from jax.sharding import PartitionSpec as P


def slots_of(route_blocks, experts):
    hits = (
        (route_blocks[..., None] == jnp.arange(experts, dtype=jnp.int32)).astype(jnp.int32).sum(2)
    )
    before = jnp.cumsum(hits, axis=1) - hits
    return jnp.take_along_axis(before, route_blocks, axis=2)


def body(grad_out, route_ids, route_probs, hidden, w_down):
    groups = lax.axis_size("expert")
    held = w_down.shape[0]
    experts = groups * held
    capacity = hidden.shape[3]
    chosen = route_ids.shape[1]
    tokens_here = grad_out.shape[0]
    features = grad_out.shape[1]
    total = jnp.sum(route_probs, axis=1, keepdims=True)
    gates = route_probs / total
    gate_word = gates.astype(jnp.bfloat16)
    slot = slots_of(route_ids[None], experts)[0]
    flat = (route_ids * capacity + slot).reshape(-1)
    send_rows = (
        jnp.zeros((experts * capacity, features), jnp.bfloat16)
        .at[flat]
        .set(jnp.repeat(grad_out, chosen, axis=0))
    )
    send_gates = jnp.zeros((experts * capacity,), jnp.bfloat16).at[flat].set(gate_word.reshape(-1))
    recv_rows, recv_gates = (
        lax.all_to_all(
            send_rows.reshape(groups, held, capacity, features),
            "expert",
            split_axis=0,
            concat_axis=0,
            tiled=True,
        ),
        lax.all_to_all(
            send_gates.reshape(groups, held, capacity),
            "expert",
            split_axis=0,
            concat_axis=0,
            tiled=True,
        ),
    )
    saved = hidden[0]
    factor = recv_gates.astype(jnp.float32)[..., None]
    raw = jnp.einsum("secd,ehd->sech", recv_rows, w_down, preferred_element_type=jnp.float32)
    hidden_grad = (factor * raw).astype(jnp.bfloat16)[None]
    gate_grad = jnp.sum(raw * saved.astype(jnp.float32), axis=-1)
    returned = lax.all_to_all(gate_grad, "expert", split_axis=0, concat_axis=0, tiled=True).reshape(
        -1
    )
    picked_grad = returned[flat].reshape(tokens_here, chosen)
    prob_grad = (picked_grad - jnp.sum(gates * picked_grad, axis=1, keepdims=True)) / total
    scaled = (factor * recv_rows.astype(jnp.float32)).astype(jnp.bfloat16)
    weight_term = jnp.einsum("sech,secd->hed", saved, scaled, preferred_element_type=jnp.float32)
    weight_grad = lax.psum_scatter(
        weight_term.astype(jnp.bfloat16), "dp", scatter_dimension=0, tiled=True
    ).astype(jnp.float32)
    return (hidden_grad, prob_grad, weight_grad)


def solution(mesh):
    in_specs = (
        P(("dp", "expert"), None),
        P(("dp", "expert"), None),
        P(("dp", "expert"), None),
        P("dp", None, "expert", None, None),
        P("expert", None, None),
    )
    out_specs = (
        P("dp", None, "expert", None, None),
        P(("dp", "expert"), None),
        P("dp", "expert", None),
    )
    return jax.shard_map(body, mesh=mesh, in_specs=in_specs, out_specs=out_specs, check_vma=False)
```

profile of v0, /device:TPU:14, one launch (start us, length us, event | category | flops | bytes accessed | tf_op | source)
XLA Modules:
  0.0 279.4 jit_solution(7363687588240118808)
XLA Ops:
  7.2 0.8 convert_reduce_fusion
  8.0 0.7 bitcast_or_fusion
  8.6 0.2 reduce_window_sum.11
  8.8 0.1 copy.78
  8.9 0.1 reshape.127
  9.1 0.0 copy-start.1
  9.1 0.0 copy-start.2
  9.1 0.0 copy-start
  9.1 1.9 gather_fusion.1
  11.0 0.1 gather.10
  11.2 0.1 copy.79
  11.3 0.1 copy.80
  11.4 0.1 reshape.110
  11.5 0.1 copy.81
  11.7 0.1 fusion.12
  11.8 0.1 reshape.137
  11.9 2.2 scatter_custom_fusion
  14.1 0.7 reshape.112
  14.8 22.8 %all-to-all-start = ((bf16[64,2,4]{2,1,0:T(2,128)(2,1)}), bf16[64,2,4]{2,1,0:T(2,128)(2,1)S(1)}, u32[]{:S(2)}, u32[]{:S(2)}) async-start(bf16[64,2,4]{2,1,0:T(2,128)(2,1)} %reshape.112), calls=%async_computation | async-start | bytes 65536 | tf_op jit(solution)/shard_map/all_to_all | solution.py:42
  37.6 0.6 broadcast_in_dim.29
  38.3 0.4 reshape.145
  38.7 2.8 %scatter_custom_fusion.1 = bf16[512,2048]{1,0:T(8,128)(2,1)S(1)} fusion(s32[256]{0:T(256)S(1)} %bitcast.41, bf16[256,2048]{1,0:T(8,128)(2,1)S(1)} %reshape.145, bf16[]{:T(256)} %constant.9.clone.1), kind=kCustom, calls=%fused_computation.15 | custom fusion | bytes 2097154 | tf_op jit(solution)/shard_map/scatter | solution.py:31
  41.5 2.2 reshape.114
  43.8 3.2 %all-to-all-done = bf16[64,2,4]{2,1,0:T(2,128)(2,1)S(1)} async-done(((bf16[64,2,4]{2,1,0:T(2,128)(2,1)}), bf16[64,2,4]{2,1,0:T(2,128)(2,1)S(1)}, u32[]{:S(2)}, u32[]{:S(2)}) %all-to-all-start) | async-done | bytes 1056 | tf_op jit(solution)/shard_map/all_to_all | solution.py:42
  47.0 9.5 %all-to-all-start.1 = ((bf16[64,2,4,2048]{3,2,1,0:T(4,128)(2,1)}), bf16[64,2,4,2048]{3,2,1,0:T(4,128)(2,1)S(1)}, u32[]{:S(2)}, u32[]{:S(2)}) async-start(bf16[64,2,4,2048]{3,2,1,0:T(4,128)(2,1)} %reshape.114), calls=%async_computation.1 | async-start | bytes 4194304 | tf_op jit(solution)/shard_map/all_to_all | solution.py:35
  56.5 0.2 all-reduce.3.cloned.1.call-start
  56.7 0.0 copy-start.3
  56.7 50.8 %all-to-all-done.1 = bf16[64,2,4,2048]{3,2,1,0:T(4,128)(2,1)S(1)} async-done(((bf16[64,2,4,2048]{3,2,1,0:T(4,128)(2,1)}), bf16[64,2,4,2048]{3,2,1,0:T(4,128)(2,1)S(1)}, u32[]{:S(2)}, u32[]{:S(2)}) %all-to-all-start.1) | async-done | bytes 2097184 | tf_op jit(solution)/shard_map/all_to_all | solution.py:35
  107.6 0.9 multiply_convert_fusion
  108.4 0.0 copy-done.3
  108.5 5.2 %fusion = bf16[768,2,2048]{0,2,1:T(8,128)(2,1)} fusion(bf16[64,2,4,2048]{3,2,1,0:T(4,128)(2,1)S(1)} %multiply_convert_fusion, bf16[1,64,2,4,768]{4,3,2,1,0:T(4,128)(2,1)S(1)} %copy-done.3), kind=kOutput, calls=%fused_computation.5 | convolution fusion | flops 1613758464 | bytes 9175040 | tf_op jit(solution)/shard_map/sech,secd->hed/dot_general | solution.py:61
  113.7 16.4 %copy.87 = bf16[768,2,2048]{2,1,0:T(2,128)(2,1)} copy(bf16[768,2,2048]{0,2,1:T(8,128)(2,1)} %fusion) | data formatting | bytes 12582912 | tf_op jit(solution)/shard_map/convert_element_type | solution.py:63
  130.1 0.0 all-reduce.3.cloned.1.call-update
  130.1 0.1 copy.82
  130.2 5.9 %fusion.6 = (f32[64,2,4]{0,2,1:T(4,128)S(1)}, bf16[1,64,2,4,768]{4,1,3,2,0:T(8,128)(2,1)S(1)}) fusion(bf16[1,64,2,4,768]{4,3,2,1,0:T(4,128)(2,1)} %param.8, f32[64,2,4]{0,2,1:T(4,128)S(1)} %copy.82, bf16[2,768,2048]{2,1,0:T(8,128)(2,1)} %param.9, bf16[64,2,4,2048]{3,2,1,0:T(4,128)(2,1)S(1)} %all-to-all-done.1), kind=kOutput, calls=%fused_computation.14 | convolution fusion | flops 1612578304 | bytes 9965568 | tf_op jit(solution)/shard_map/secd,ehd->sech/dot_general | solution.py:52
  136.1 0.7 copy.85
  136.8 12.0 %all-to-all-start.2 = ((f32[64,2,4]{2,1,0:T(2,128)}), f32[64,2,4]{2,1,0:T(2,128)S(1)}, u32[]{:S(2)}, u32[]{:S(2)}) async-start(f32[64,2,4]{2,1,0:T(2,128)} %copy.85), calls=%async_computation.2 | async-start | bytes 131072 | tf_op jit(solution)/shard_map/all_to_all | solution.py:55
  148.9 1.3 dynamic-slice
  150.8 1.5 copy.88
  152.3 6.1 %all-to-all-done.2 = f32[64,2,4]{2,1,0:T(2,128)S(1)} async-done(((f32[64,2,4]{2,1,0:T(2,128)}), f32[64,2,4]{2,1,0:T(2,128)S(1)}, u32[]{:S(2)}, u32[]{:S(2)}) %all-to-all-start.2) | async-done | bytes 2080 | tf_op jit(solution)/shard_map/all_to_all | solution.py:55
  158.4 0.1 reshape.115
  158.6 2.0 gather_fusion
  160.5 0.1 reshape.116
  160.7 0.2 multiply_reduce_fusion
  160.9 0.1 subtract_divide_fusion
  161.0 0.6 copy.89
  161.6 108.6 %all-reduce.3.cloned.1.call-done = bf16[768,2,2048]{2,1,0:T(2,128)(2,1)} async-done(((bf16[768,2,2048]{2,1,0:T(2,128)(2,1)}), bf16[768,2,2048]{2,1,0:T(2,128)(2,1)}) %all-reduce.3.cloned.1.call-update) | async-done | bytes 6291472
  270.2 2.3 dynamic-slice_convert_fusion
  (9 shorter events, 0.1 us)
Async XLA Ops:
  9.1 2.1 copy-start.1
  9.1 2.4 copy-start.2
  9.1 28.5 %copy-start = (bf16[128,2048]{1,0:T(8,128)(2,1)S(1)}, bf16[128,2048]{1,0:T(8,128)(2,1)}, u32[]{:S(2)}) copy-start(bf16[128,2048]{1,0:T(8,128)(2,1)} %param.5) | copy-start | bytes 1572868
  14.8 32.2 %all-to-all-start = ((bf16[64,2,4]{2,1,0:T(2,128)(2,1)}), bf16[64,2,4]{2,1,0:T(2,128)(2,1)S(1)}, u32[]{:S(2)}, u32[]{:S(2)}) async-start(bf16[64,2,4]{2,1,0:T(2,128)(2,1)} %reshape.112), calls=%async_computation | async-start | bytes 65536 | tf_op jit(solution)/shard_map/all_to_all | solution.py:42
  47.0 60.6 %all-to-all-start.1 = ((bf16[64,2,4,2048]{3,2,1,0:T(4,128)(2,1)}), bf16[64,2,4,2048]{3,2,1,0:T(4,128)(2,1)S(1)}, u32[]{:S(2)}, u32[]{:S(2)}) async-start(bf16[64,2,4,2048]{3,2,1,0:T(4,128)(2,1)} %reshape.114), calls=%async_computation.1 | async-start | bytes 4194304 | tf_op jit(solution)/shard_map/all_to_all | solution.py:35
  56.5 213.8 %all-reduce.3.cloned.1.call-start = ((), (), s32[]{:S(2)}) async-start(), calls=%async_computation.3 | async-start | bytes 12582912
  56.7 51.7 %copy-start.3 = (bf16[1,64,2,4,768]{4,3,2,1,0:T(4,128)(2,1)S(1)}, bf16[1,64,2,4,768]{4,3,2,1,0:T(4,128)(2,1)}, u32[]{:S(2)}) copy-start(bf16[1,64,2,4,768]{4,3,2,1,0:T(4,128)(2,1)} %param.8) | copy-start | bytes 2359300
  136.8 21.6 %all-to-all-start.2 = ((f32[64,2,4]{2,1,0:T(2,128)}), f32[64,2,4]{2,1,0:T(2,128)S(1)}, u32[]{:S(2)}, u32[]{:S(2)}) async-start(f32[64,2,4]{2,1,0:T(2,128)} %copy.85), calls=%async_computation.2 | async-start | bytes 131072 | tf_op jit(solution)/shard_map/all_to_all | solution.py:55
Sparse Core Ops, SparseCore 0:
  130.2 139.9 all-reduce.2
where the time goes:
time: 281 us; the launch traced here: 279 us
  waiting for transfers between devices  169 us (60%)
  starting transfers between devices  44.5 us (16%)
  local copies, waits for them, and re-layouts  34.7 us (12%)
  between operations  14.9 us (5%)
  matrix products  11.1 us (4%)
  other arithmetic  5.31 us (2%)
    unnamed x2, waiting for transfers between devices  109 us
    all_to_all x1, waiting for transfers between devices, body(): lax.all_to_all(send_rows.reshape(groups, held, capacity, features), 'expe...  50.8 us
    all_to_all x1, starting transfers between devices, body(): lax.all_to_all(send_gates.reshape(groups, held, capacity), 'expert', spli...  22.8 us
    convert_element_type x1, local copies, waits for them, and re-layouts, body(): weight_term.astype(jnp.bfloat16)  16.4 us
    all_to_all x1, starting transfers between devices, body(): lax.all_to_all(gate_grad, 'expert', split_axis=0, concat_axis=0, tiled=True)  12 us
    all_to_all x1, starting transfers between devices, body(): lax.all_to_all(send_rows.reshape(groups, held, capacity, features), 'expe...  9.5 us
    all_to_all x1, waiting for transfers between devices, body(): lax.all_to_all(gate_grad, 'expert', split_axis=0, concat_axis=0, tiled=True)  6.13 us
    dot_general x1, matrix products, body(): jnp.einsum('secd,ehd->sech', recv_rows, w_down, preferred_element_type=jn...  5.88 us
  transfers between devices with their start and end apart: 4, of which 4 were waited for; matrix products, arithmetic and copies ran while one was open for 7% of the time, Pallas kernels for 0%

commit v1 on v0

v1 whole, which is shorter than its diff:
```python
import functools

import jax
import jax.numpy as jnp
from jax import lax
from jax.experimental import pallas as pl
from jax.experimental.pallas import tpu as pltpu
from jax.sharding import PartitionSpec as P

MESH = pl.DeviceIdType.MESH
F32 = jnp.float32
BF16 = jnp.bfloat16
WIDTHS = (512, 512, 512, 512)
STARTS = tuple(sum(WIDTHS[:i]) for i in range(len(WIDTHS)))
CHUNKS = len(WIDTHS)
SIDE = 8
GROUPS = 64
SLOTS = 8
TOK = 128
H = 768
D = 2048
PART = 48


def kernel(
    grad_ref, ids_ref, probs_ref, hid_ref, w_ref,
    hg_ref, prob_ref, wg_ref,
    grad, wv, hid, hid_t, pick, rows, acc, hg, ret_out, ret_in, ret,
    send, recv, term, sib, out_buf, in_buf, wg,
    load_sem, a2a_send, a2a_recv, own_sem, sib_send, sib_recv, ring_send, ring_recv,
    ret_send, ret_recv, ret_own, store_sem,
):
    me = lax.axis_index("expert")
    dp = lax.axis_index("dp")
    mx, mz = me // SIDE, me % SIDE
    core = dp % 2
    y = dp // 2
    twin = dp + 1 - 2 * core
    ways = ((dp + 2) % 16, (dp + 14) % 16)

    def peer(k):
        dx, dz = k % SIDE, (k // SIDE + k) % SIDE
        return ((mx + dx) % SIDE) * SIDE + (mz + dz) % SIDE

    loads = [
        pltpu.make_async_copy(grad_ref, grad, load_sem.at[0]),
        pltpu.make_async_copy(hid_ref, hid, load_sem.at[1]),
        pltpu.make_async_copy(w_ref, wv, load_sem.at[2]),
    ]
    for load in loads:
        load.start()

    barrier = pltpu.get_barrier_semaphore()

    def greet(k, carry):
        pl.semaphore_signal(barrier, inc=1, device_id={"expert": peer(k)}, device_id_type=MESH)
        return carry

    lax.fori_loop(1, GROUPS, greet, 0)
    for other in (twin, *ways):
        pl.semaphore_signal(barrier, inc=1, device_id={"dp": other}, device_id_type=MESH)

    ids = [ids_ref[k : k + 1, :] for k in range(2)]
    probs = [probs_ref[k : k + 1, :] for k in range(2)]
    total = probs[0] + probs[1]
    gates = [p / total for p in probs]
    words = [g.astype(BF16).astype(F32) for g in gates]
    named = lax.broadcasted_iota(jnp.int32, (2 * GROUPS, TOK), 0)
    is_expert = [(named == i).astype(F32) for i in ids]
    earlier = (
        lax.broadcasted_iota(jnp.int32, (TOK, TOK), 0) < lax.broadcasted_iota(jnp.int32, (TOK, TOK), 1)
    ).astype(F32)
    before = jnp.dot(
        (is_expert[0] + is_expert[1]).astype(BF16), earlier.astype(BF16), preferred_element_type=F32
    )
    slot = [jnp.sum(before * i, axis=0, keepdims=True).astype(jnp.int32) for i in is_expert]
    place = [i * 4 + s for i, s in zip(ids, slot)]
    where = lax.broadcasted_iota(jnp.int32, (GROUPS * SLOTS, TOK), 0)
    pick[...] = (
        jnp.where(where == place[0], words[0], 0.0) + jnp.where(where == place[1], words[1], 0.0)
    ).astype(BF16)

    loads[0].wait()

    def fill(c):
        cols = slice(STARTS[c], STARTS[c] + WIDTHS[c])

        def group(i, carry):
            at = pl.multiple_of(i * 128, 128)
            got = jnp.dot(pick[pl.ds(at, 128), :], grad[:, cols], preferred_element_type=F32)
            send[c][pl.ds(i * 16, 16)] = got.reshape(16, SLOTS, WIDTHS[c]).astype(BF16)
            return carry

        lax.fori_loop(0, 4, group, 0)

    def launch(c):
        def one(k, carry):
            to = peer(k)
            pltpu.make_async_remote_copy(
                send[c].at[to], recv[c].at[me], a2a_send.at[c], a2a_recv.at[c],
                device_id={"expert": to}, device_id_type=MESH,
            ).start()
            return carry

        lax.fori_loop(1, GROUPS, one, 0)
        pltpu.make_async_copy(send[c].at[me], recv[c].at[me], own_sem.at[c]).start()

    def all_pairs(c):
        return pltpu.make_async_remote_copy(
            send[c].at[pl.ds(0, GROUPS - 1)], recv[c].at[pl.ds(0, GROUPS - 1)], a2a_send.at[c], a2a_recv.at[c],
            device_id={"expert": me}, device_id_type=MESH,
        )

    fill(0)
    pl.semaphore_wait(barrier, GROUPS - 1 + 3)
    launch(0)
    for c in range(1, CHUNKS):
        fill(c)
        launch(c)

    loads[1].wait()

    def turn(i, carry):
        at = pl.multiple_of(i * 128, 128)
        for e in range(2):
            hid_t[e, pl.ds(at, 128), :] = hid[e, :, pl.ds(at, 128)].astype(F32).T.astype(BF16)
        return carry

    lax.fori_loop(0, H // 128, turn, 0)
    loads[2].wait()

    def arrive(c):
        all_pairs(c).wait_recv()
        pltpu.make_async_copy(send[c].at[me], recv[c].at[me], own_sem.at[c]).wait()

    low = lax.broadcasted_iota(jnp.int32, (32, 8, 128), 1) < 4

    def part(c):
        def tile(n, carry):
            at = pl.multiple_of(n * 128, 128)
            got = recv[c][:, :, pl.ds(at, 128)].astype(F32).reshape(32, 2, 8, 128)
            even, odd = got[:, 0], got[:, 1]
            first = jnp.where(low, even, pltpu.roll(odd, 4, 1))
            second = jnp.where(low, pltpu.roll(even, 4, 1), odd)
            rows[0, :, pl.ds(at, 128)] = first.reshape(256, 128).astype(BF16)
            rows[1, :, pl.ds(at, 128)] = second.reshape(256, 128).astype(BF16)
            return carry

        lax.fori_loop(0, WIDTHS[c] // 128, tile, 0)

    def twin_copy(c, e):
        return pltpu.make_async_remote_copy(
            term[c].at[e, :, 1 - core], sib[c].at[e], sib_send.at[c, e], sib_recv.at[c, e],
            device_id={"dp": twin}, device_id_type=MESH,
        )

    def terms(c):
        for e in range(2):
            def tile(n, carry):
                at = pl.multiple_of(n * 256, 256)
                for m in range(2):
                    got = jnp.dot(
                        hid_t[e, m * 384 : (m + 1) * 384, :], rows[e, :, pl.ds(at, 256)], preferred_element_type=F32
                    )
                    term[c][e, m * 4 : (m + 1) * 4, :, :, pl.ds(at, 256)] = got.astype(BF16).reshape(4, 2, PART, 256)
                return carry

            lax.fori_loop(0, WIDTHS[c] // 256, tile, 0)
            twin_copy(c, e).start()

    def raws(c):
        cols = slice(STARTS[c], STARTS[c] + WIDTHS[c])
        for e in range(2):
            def tile(j, carry):
                at = pl.multiple_of(j * 256, 256)
                got = lax.dot_general(
                    rows[e, :, 0 : WIDTHS[c]], wv[e, pl.ds(at, 256), cols], (((1,), (1,)), ((), ())),
                    preferred_element_type=F32,
                )
                if c == 0:
                    acc[e, :, pl.ds(at, 256)] = got
                else:
                    acc[e, :, pl.ds(at, 256)] += got
                return carry

            lax.fori_loop(0, H // 256, tile, 0)

    def ring_copy(c, way, step):
        span = pl.ds(way, 1) if step == 0 else pl.ds(0, 2)
        return pltpu.make_async_remote_copy(
            out_buf[c].at[way, step, span], in_buf[c].at[way, step, span],
            ring_send.at[c, way, step], ring_recv.at[c, way, step],
            device_id={"dp": ways[way]}, device_id_type=MESH,
        )

    def chip_sum(c, e, at):
        return term[c][e, at, core].astype(F32) + sib[c][e, at].astype(F32)

    def ring(c, step):
        if step == 0:
            for e in range(2):
                twin_copy(c, e).wait_recv()
        for way in range(2):
            if step > 0:
                ring_copy(c, way, step - 1).wait_recv()
            target = (y + 4 - step) % SIDE if way == 0 else (y + 4 + step) % SIDE
            for e in range(2):
                if step == 0 and e != way:
                    continue
                value = chip_sum(c, e, target)
                if step > 1 or (step == 1 and e == way):
                    value = value + in_buf[c][way, step - 1, e].astype(F32)
                out_buf[c][way, step, e] = value.astype(BF16)
            ring_copy(c, way, step).start()

    def store_wg(c):
        cols = pl.ds(STARTS[c], WIDTHS[c])
        return pltpu.make_async_copy(wg.at[:, :, cols], wg_ref.at[:, :, cols], store_sem.at[c])

    def finish(c):
        for way in range(2):
            ring_copy(c, way, 3).wait_recv()
        for e in range(2):
            value = chip_sum(c, e, y) + in_buf[c][0, 3, e].astype(F32) + in_buf[c][1, 3, e].astype(F32)
            wg[e, :, STARTS[c] : STARTS[c] + WIDTHS[c]] = value
        store_wg(c).start()

    def ret_copies():
        return pltpu.make_async_remote_copy(
            ret_out.at[pl.ds(0, GROUPS - 1)], ret_in.at[pl.ds(0, GROUPS - 1)], ret_send, ret_recv,
            device_id={"expert": me}, device_id_type=MESH,
        )

    def store_hg():
        return pltpu.make_async_copy(hg, hg_ref, store_sem.at[CHUNKS])

    def answer():
        row = lax.broadcasted_iota(jnp.int32, (256, 128), 0)
        lane = lax.broadcasted_iota(jnp.int32, (256, 128), 1)
        source = lax.broadcasted_iota(jnp.int32, (GROUPS, 256), 0)
        of_source = (lax.broadcasted_iota(jnp.int32, (GROUPS, 256), 1) // 4 == source).astype(F32)
        both = jnp.zeros((GROUPS, 128), F32)
        for e in range(2):
            dots = jnp.sum(acc[e] * hid[e].astype(F32), axis=1, keepdims=True)
            spread = jnp.where(lane == 4 * e + row % 4, dots, 0.0)
            both = both + jnp.dot(
                of_source, spread, preferred_element_type=F32, precision=lax.Precision.HIGHEST
            )
            hg[e] = acc[e].astype(BF16)
        for g in range(GROUPS):
            ret_out[g] = both[g : g + 1, :]

        def one(k, carry):
            to = peer(k)
            pltpu.make_async_remote_copy(
                ret_out.at[to], ret_in.at[me], ret_send, ret_recv, device_id={"expert": to}, device_id_type=MESH
            ).start()
            return carry

        lax.fori_loop(1, GROUPS, one, 0)
        pltpu.make_async_copy(ret_out.at[me], ret_in.at[me], ret_own).start()
        store_hg().start()

    def gate_gradients():
        ret_copies().wait_recv()
        pltpu.make_async_copy(ret_out.at[me], ret_in.at[me], ret_own).wait()
        for g in range(GROUPS):
            ret[g : g + 1, :] = ret_in[g]
        got = ret[...]
        group = lax.broadcasted_iota(jnp.int32, (GROUPS, TOK), 0)
        lane = lax.broadcasted_iota(jnp.int32, (128, TOK), 0)
        picked = []
        for k in range(2):
            here = (group == place[k] // SLOTS).astype(F32)
            wide = lax.dot_general(
                got, here, (((0,), (0,)), ((), ())), preferred_element_type=F32, precision=lax.Precision.HIGHEST
            )
            scaled = jnp.sum(jnp.where(lane == place[k] % SLOTS, wide, 0.0), axis=0, keepdims=True)
            picked.append(scaled / words[k])
        mean = gates[0] * picked[0] + gates[1] * picked[1]
        for k in range(2):
            prob_ref[k : k + 1, :] = (picked[k] - mean) / total

    def work(c):
        arrive(c)
        part(c)
        terms(c)
        raws(c)

    last = CHUNKS - 1
    work(0)
    for c in range(1, CHUNKS):
        for step in range(3):
            ring(c - 1, step)
        work(c)
        ring(c - 1, 3)
        if c < last:
            finish(c - 1)
    ring(last, 0)
    answer()
    finish(last - 1)
    for step in range(1, 4):
        ring(last, step)
    gate_gradients()
    finish(last)

    for c in range(CHUNKS):
        all_pairs(c).wait_send()
        for e in range(2):
            twin_copy(c, e).wait_send()
        for way in range(2):
            for step in range(4):
                ring_copy(c, way, step).wait_send()
        store_wg(c).wait()
    ret_copies().wait_send()
    store_hg().wait()


def body(grad_out, route_ids, route_probs, hidden, w_down):
    hid = hidden[0].transpose(1, 0, 2, 3).reshape(2, 256, H)
    any_space = pl.BlockSpec(memory_space=pl.ANY)
    vmem = pl.BlockSpec(memory_space=pltpu.VMEM)
    dma = pltpu.SemaphoreType.DMA
    hg, prob, wg = pl.pallas_call(
        kernel,
        out_shape=(
            jax.ShapeDtypeStruct((2, 256, H), BF16),
            jax.ShapeDtypeStruct((2, TOK), F32),
            jax.ShapeDtypeStruct((2, PART, D), F32),
        ),
        in_specs=[any_space, vmem, vmem, any_space, any_space],
        out_specs=(any_space, vmem, any_space),
        scratch_shapes=[
            pltpu.VMEM((TOK, D), BF16),
            pltpu.VMEM((2, H, D), BF16),
            pltpu.VMEM((2, 256, H), BF16),
            pltpu.VMEM((2, H, 256), BF16),
            pltpu.VMEM((GROUPS * SLOTS, TOK), BF16),
            pltpu.VMEM((2, 256, max(WIDTHS)), BF16),
            pltpu.VMEM((2, 256, H), F32),
            pltpu.VMEM((2, 256, H), BF16),
            pltpu.VMEM((GROUPS, 1, 128), F32),
            pltpu.VMEM((GROUPS, 1, 128), F32),
            pltpu.VMEM((GROUPS, 128), F32),
            [pltpu.VMEM((GROUPS, SLOTS, w), BF16) for w in WIDTHS],
            [pltpu.VMEM((GROUPS, SLOTS, w), BF16) for w in WIDTHS],
            [pltpu.VMEM((2, SIDE, 2, PART, w), BF16) for w in WIDTHS],
            [pltpu.VMEM((2, SIDE, PART, w), BF16) for w in WIDTHS],
            [pltpu.VMEM((2, 4, 2, PART, w), BF16) for w in WIDTHS],
            [pltpu.VMEM((2, 4, 2, PART, w), BF16) for w in WIDTHS],
            pltpu.VMEM((2, PART, D), F32),
            dma((3,)),
            dma((CHUNKS,)),
            dma((CHUNKS,)),
            dma((CHUNKS,)),
            dma((CHUNKS, 2)),
            dma((CHUNKS, 2)),
            dma((CHUNKS, 2, 4)),
            dma((CHUNKS, 2, 4)),
            dma,
            dma,
            dma,
            dma((CHUNKS + 1,)),
        ],
        compiler_params=pltpu.CompilerParams(
            collective_id=0, has_side_effects=True, vmem_limit_bytes=56 * 2**20
        ),
        name="routed_backward",
    )(grad_out, route_ids.T, route_probs.T, hid, w_down)
    hidden_grad = hg.reshape(2, GROUPS, 4, H).transpose(1, 0, 2, 3)[None]
    return hidden_grad, prob.T, wg.transpose(1, 0, 2)


def solution(mesh):
    in_specs = (
        P(("dp", "expert"), None),
        P(("dp", "expert"), None),
        P(("dp", "expert"), None),
        P("dp", None, "expert", None, None),
        P("expert", None, None),
    )
    out_specs = (
        P("dp", None, "expert", None, None),
        P(("dp", "expert"), None),
        P("dp", "expert", None),
    )
    return jax.shard_map(body, mesh=mesh, in_specs=in_specs, out_specs=out_specs, check_vma=False)
```

time: 281 us -> 122 us (0.43)
  the two profiles are of different devices: /device:TPU:14 before, /device:TPU:128 now
where the time goes in v1:
time: 122 us; the launch traced here: 121 us
  Pallas kernels  112 us (92%)
  local copies, waits for them, and re-layouts  9.16 us (8%)
    pallas_call x1, Pallas kernels, body(): pl.pallas_call(kernel, out_shape=(jax.ShapeDtypeStruct((2, 256, H), BF16)...  112 us
    unnamed x2, local copies, waits for them, and re-layouts  3.85 us
    reshape x2, local copies, waits for them, and re-layouts, body(): hidden_grad = hg.reshape(2, GROUPS, 4, H).transpose(1, 0, 2, 3)[None]  2.84 us

profile of v1, /device:TPU:128, one launch (start us, length us, event | category | flops | bytes accessed | tf_op | source)
XLA Modules:
  0.0 121.4 jit_solution(4985360585381439799)
XLA Ops:
  0.6 1.4 %copy.8 = bf16[2,64,4,768]{3,2,1,0:T(4,128)(2,1)S(1)} copy(bf16[2,64,4,768]{3,2,0,1:T(4,128)(2,1)} %bitcast.12) | data formatting | bytes 1572864 | tf_op jit(solution)/shard_map/transpose | solution.py:320
  2.0 1.1 reshape.12.hid_ref
  3.1 111.6 %routed_backward.1 = (bf16[2,256,768]{2,1,0:T(8,128)(2,1)}, f32[2,128]{1,0:T(2,128)}, f32[2,48,2048]{2,1,0:T(8,128)}) custom-call(bf16[128,2048]{1,0:T(8,128)(2,1)} %grad_ref.1, s32[2,128]{1,0:T(2,128)} %bitcast.15, f32[2,128]{1,0:T(2,128)} %bitcast.16, bf16[2,256,768]{2,1,0:T(8,128)(2,1)} %reshape.12.hid_ref, bf16[2,768,2048]{2,1,0:T(8,128)(2,1)} %w_ref.1), custom_call_target="tpu_custom_call" | custom-call | tf_op jit(solution)/shard_map/routed_backward/pallas_call | solution.py:324
  114.7 1.7 %reshape.13 = bf16[2,64,4,768]{3,2,1,0:T(4,128)(2,1)S(1)} reshape(bf16[2,256,768]{2,1,0:T(8,128)(2,1)} %get-tuple-element.6) | data formatting | bytes 1572864 | tf_op jit(solution)/shard_map/reshape | solution.py:370
  116.4 1.2 copy.12
  117.5 2.6 %copy.10 = f32[48,2,2048]{2,1,0:T(2,128)} copy(f32[48,2,2048]{2,0,1:T(8,128)} %bitcast.14) | data formatting | bytes 1572864
  120.1 1.2 %copy.14 = f32[128,2]{0,1:T(2,128)} copy(f32[128,2]{0,1:T(2,128)} %bitcast.17) | data formatting | bytes 2048

commit v2 on v1

--- a/solution.py
+++ b/solution.py
@@ -1,5 +1,3 @@
-import functools
-
 import jax
 import jax.numpy as jnp
 from jax import lax
@@ -13,6 +11,10 @@
 WIDTHS = (512, 512, 512, 512)
 STARTS = tuple(sum(WIDTHS[:i]) for i in range(len(WIDTHS)))
 CHUNKS = len(WIDTHS)
+UNITS = ((0, 0, 512), (1, 0, 512), (2, 0, 512), (3, 0, 256), (3, 256, 256))
+WINDOW = 8
+BATCHES = tuple((c, k, k + 4096 // w) for c, w in enumerate(WIDTHS) for k in range(0, 64, 4096 // w))
+ENDS = tuple(sum(w // 64 for w in WIDTHS[: c + 1]) for c in range(len(WIDTHS)))
 SIDE = 8
 GROUPS = 64
 SLOTS = 8
@@ -25,9 +27,9 @@
 def kernel(
     grad_ref, ids_ref, probs_ref, hid_ref, w_ref,
     hg_ref, prob_ref, wg_ref,
-    grad, wv, hid, hid_t, pick, rows, acc, hg, ret_out, ret_in, ret,
+    grad, wv, hid_raw, hid, hid_t, pick, rows, acc, hg, ret_out, ret_in, ret,
     send, recv, term, sib, out_buf, in_buf, wg,
-    load_sem, a2a_send, a2a_recv, own_sem, sib_send, sib_recv, ring_send, ring_recv,
+    load_sem, a2a_send, a2a_recv, own_sem, sib_send, sib_recv, hop_send, hop_recv,
     ret_send, ret_recv, ret_own, store_sem,
 ):
     me = lax.axis_index("expert")
@@ -36,7 +38,7 @@
     core = dp % 2
     y = dp // 2
     twin = dp + 1 - 2 * core
-    ways = ((dp + 2) % 16, (dp + 14) % 16)
+    ways = (((dp + 2) % 16, (dp + 4) % 16), ((dp + 14) % 16, (dp + 12) % 16))
 
     def peer(k):
         dx, dz = k % SIDE, (k // SIDE + k) % SIDE
@@ -44,7 +46,7 @@
 
     loads = [
         pltpu.make_async_copy(grad_ref, grad, load_sem.at[0]),
-        pltpu.make_async_copy(hid_ref, hid, load_sem.at[1]),
+        pltpu.make_async_copy(hid_ref, hid_raw, load_sem.at[1]),
         pltpu.make_async_copy(w_ref, wv, load_sem.at[2]),
     ]
     for load in loads:
@@ -57,7 +59,7 @@
         return carry
 
     lax.fori_loop(1, GROUPS, greet, 0)
-    for other in (twin, *ways):
+    for other in (twin, *ways[0], *ways[1]):
         pl.semaphore_signal(barrier, inc=1, device_id={"dp": other}, device_id_type=MESH)
 
     ids = [ids_ref[k : k + 1, :] for k in range(2)]
@@ -93,32 +95,56 @@
 
         lax.fori_loop(0, 4, group, 0)
 
-    def launch(c):
-        def one(k, carry):
-            to = peer(k)
-            pltpu.make_async_remote_copy(
-                send[c].at[to], recv[c].at[me], a2a_send.at[c], a2a_recv.at[c],
-                device_id={"expert": to}, device_id_type=MESH,
-            ).start()
-            return carry
-
-        lax.fori_loop(1, GROUPS, one, 0)
-        pltpu.make_async_copy(send[c].at[me], recv[c].at[me], own_sem.at[c]).start()
-
-    def all_pairs(c):
+    def pairs(c, b, count):
         return pltpu.make_async_remote_copy(
-            send[c].at[pl.ds(0, GROUPS - 1)], recv[c].at[pl.ds(0, GROUPS - 1)], a2a_send.at[c], a2a_recv.at[c],
+            send[c].at[pl.ds(0, count)], recv[c].at[pl.ds(0, count)], a2a_send.at[b], a2a_recv.at[c],
             device_id={"expert": me}, device_id_type=MESH,
         )
 
+    def drain(b):
+        c, start, stop = BATCHES[b]
+        pairs(c, b, stop - max(start, 1)).wait_send()
+
+    issued = [0]
+
+    def pump(count=1):
+        for _ in range(count):
+            b = issued[0]
+            if b == len(BATCHES):
+                return
+            issued[0] = b + 1
+            if b >= WINDOW:
+                drain(b - WINDOW)
+            c, start, stop = BATCHES[b]
+
+            def one(k, carry):
+                to = peer(k)
+                pltpu.make_async_remote_copy(
+                    send[c].at[to], recv[c].at[me], a2a_send.at[b], a2a_recv.at[c],
+                    device_id={"expert": to}, device_id_type=MESH,
+                ).start()
+                return carry
+
+            lax.fori_loop(max(1, start), stop, one, 0)
+            if start == 0:
+                pltpu.make_async_copy(send[c].at[me], recv[c].at[me], own_sem.at[c]).start()
+
     fill(0)
-    pl.semaphore_wait(barrier, GROUPS - 1 + 3)
-    launch(0)
+    pl.semaphore_wait(barrier, GROUPS - 1 + 5)
+    pump(WINDOW)
     for c in range(1, CHUNKS):
         fill(c)
-        launch(c)
+        pump()
 
     loads[1].wait()
+
+    def expand(i, carry):
+        for e in range(2):
+            four = [hid_raw[4 * i + j, e].astype(F32) for j in range(4)]
+            hid[e, pl.ds(pl.multiple_of(16 * i, 16), 16), :] = jnp.concatenate(four, axis=0).astype(BF16)
+        return carry
+
+    lax.fori_loop(0, GROUPS // 4, expand, 0)
 
     def turn(i, carry):
         at = pl.multiple_of(i * 128, 128)
@@ -128,9 +154,10 @@
 
     lax.fori_loop(0, H // 128, turn, 0)
     loads[2].wait()
+    pump(ENDS[0] + WINDOW - issued[0])
 
     def arrive(c):
-        all_pairs(c).wait_recv()
+        pairs(c, 0, GROUPS - 1).wait_recv()
         pltpu.make_async_copy(send[c].at[me], recv[c].at[me], own_sem.at[c]).wait()
 
     low = lax.broadcasted_iota(jnp.int32, (32, 8, 128), 1) < 4
@@ -154,19 +181,19 @@
             device_id={"dp": twin}, device_id_type=MESH,
         )
 
-    def terms(c):
-        for e in range(2):
-            def tile(n, carry):
-                at = pl.multiple_of(n * 256, 256)
-                for m in range(2):
-                    got = jnp.dot(
-                        hid_t[e, m * 384 : (m + 1) * 384, :], rows[e, :, pl.ds(at, 256)], preferred_element_type=F32
-                    )
-                    term[c][e, m * 4 : (m + 1) * 4, :, :, pl.ds(at, 256)] = got.astype(BF16).reshape(4, 2, PART, 256)
+    def terms(u):
+        _, first, size = UNITS[u]
+        for e in range(2):
+            def tile(m, carry):
+                got = jnp.dot(
+                    hid_t[e, pl.ds(pl.multiple_of(m * 384, 384), 384), :], rows[e, :, first : first + size],
+                    preferred_element_type=F32,
+                )
+                term[u][e, pl.ds(m * 4, 4)] = got.astype(BF16).reshape(4, 2, PART, size)
                 return carry
 
-            lax.fori_loop(0, WIDTHS[c] // 256, tile, 0)
-            twin_copy(c, e).start()
+            lax.fori_loop(0, 2, tile, 0)
+            twin_copy(u, e).start()
 
     def raws(c):
         cols = slice(STARTS[c], STARTS[c] + WIDTHS[c])
@@ -185,44 +212,58 @@
 
             lax.fori_loop(0, H // 256, tile, 0)
 
-    def ring_copy(c, way, step):
-        span = pl.ds(way, 1) if step == 0 else pl.ds(0, 2)
+    def hop(u, way, kind):
+        span = pl.ds(way, 1) if kind == 0 else pl.ds(0, 2)
         return pltpu.make_async_remote_copy(
-            out_buf[c].at[way, step, span], in_buf[c].at[way, step, span],
-            ring_send.at[c, way, step], ring_recv.at[c, way, step],
-            device_id={"dp": ways[way]}, device_id_type=MESH,
+            out_buf[u].at[way, kind, span], in_buf[u].at[way, kind, span],
+            hop_send.at[u, way, kind], hop_recv.at[u, way, kind],
+            device_id={"dp": ways[way][1 if kind in (0, 3) else 0]}, device_id_type=MESH,
         )
+
+    def target(way, distance):
+        return (y + (distance if way == 0 else SIDE - distance)) % SIDE
 
     def chip_sum(c, e, at):
         return term[c][e, at, core].astype(F32) + sib[c][e, at].astype(F32)
 
-    def ring(c, step):
-        if step == 0:
+    def spread(u):
+        for e in range(2):
+            twin_copy(u, e).wait_recv()
+        for way in range(2):
+            out_buf[u][way, 0, way] = chip_sum(u, way, target(way, 4)).astype(BF16)
+            hop(u, way, 0).start()
+            for kind, distance in ((1, 3), (2, 1)):
+                for e in range(2):
+                    out_buf[u][way, kind, e] = chip_sum(u, e, target(way, distance)).astype(BF16)
+                hop(u, way, kind).start()
+
+    def gather(u):
+        for way in range(2):
+            for kind in range(2):
+                hop(u, way, kind).wait_recv()
             for e in range(2):
-                twin_copy(c, e).wait_recv()
+                value = chip_sum(u, e, target(way, 2)) + in_buf[u][way, 1, e].astype(F32)
+                if e == way:
+                    value = value + in_buf[u][way, 0, e].astype(F32)
+                out_buf[u][way, 3, e] = value.astype(BF16)
+            hop(u, way, 3).start()
+
+    def store_wg(c):
+        chunk, first, size = UNITS[c]
+        cols = pl.ds(STARTS[chunk] + first, size)
+        return pltpu.make_async_copy(wg.at[:, :, cols], wg_ref.at[:, :, cols], store_sem.at[c])
+
+    def finish(c):
+        chunk, first, size = UNITS[c]
+        start = STARTS[chunk] + first
         for way in range(2):
-            if step > 0:
-                ring_copy(c, way, step - 1).wait_recv()
-            target = (y + 4 - step) % SIDE if way == 0 else (y + 4 + step) % SIDE
-            for e in range(2):
-                if step == 0 and e != way:
-                    continue
-                value = chip_sum(c, e, target)
-                if step > 1 or (step == 1 and e == way):
-                    value = value + in_buf[c][way, step - 1, e].astype(F32)
-                out_buf[c][way, step, e] = value.astype(BF16)
-            ring_copy(c, way, step).start()
-
-    def store_wg(c):
-        cols = pl.ds(STARTS[c], WIDTHS[c])
-        return pltpu.make_async_copy(wg.at[:, :, cols], wg_ref.at[:, :, cols], store_sem.at[c])
-
-    def finish(c):
-        for way in range(2):
-            ring_copy(c, way, 3).wait_recv()
-        for e in range(2):
-            value = chip_sum(c, e, y) + in_buf[c][0, 3, e].astype(F32) + in_buf[c][1, 3, e].astype(F32)
-            wg[e, :, STARTS[c] : STARTS[c] + WIDTHS[c]] = value
+            for kind in (2, 3):
+                hop(c, way, kind).wait_recv()
+        for e in range(2):
+            value = chip_sum(c, e, y)
+            for way in range(2):
+                value = value + in_buf[c][way, 2, e].astype(F32) + in_buf[c][way, 3, e].astype(F32)
+            wg[:, e, start : start + size] = value
         store_wg(c).start()
 
     def ret_copies():
@@ -232,7 +273,7 @@
         )
 
     def store_hg():
-        return pltpu.make_async_copy(hg, hg_ref, store_sem.at[CHUNKS])
+        return pltpu.make_async_copy(hg, hg_ref, store_sem.at[len(UNITS)])
 
     def answer():
         row = lax.broadcasted_iota(jnp.int32, (256, 128), 0)
@@ -246,7 +287,6 @@
             both = both + jnp.dot(
                 of_source, spread, preferred_element_type=F32, precision=lax.Precision.HIGHEST
             )
-            hg[e] = acc[e].astype(BF16)
         for g in range(GROUPS):
             ret_out[g] = both[g : g + 1, :]
 
@@ -259,6 +299,17 @@
 
         lax.fori_loop(1, GROUPS, one, 0)
         pltpu.make_async_copy(ret_out.at[me], ret_in.at[me], ret_own).start()
+
+    def collect():
+        def eight(i, carry):
+            at = pl.multiple_of(8 * i, 8)
+            for e in range(2):
+                both = acc[e, pl.ds(at, 8), :]
+                for j in range(2):
+                    hg[2 * i + j, e] = both[4 * j : 4 * j + 4, :].astype(BF16)
+            return carry
+
+        lax.fori_loop(0, GROUPS // 2, eight, 0)
         store_hg().start()
 
     def gate_gradients():
@@ -281,94 +332,105 @@
         for k in range(2):
             prob_ref[k : k + 1, :] = (picked[k] - mean) / total
 
-    def work(c):
+    def begin(c):
+        pump(ENDS[c] + WINDOW - issued[0])
         arrive(c)
         part(c)
+
+    for c in range(3):
+        begin(c)
         terms(c)
+        pump()
         raws(c)
-
-    last = CHUNKS - 1
-    work(0)
-    for c in range(1, CHUNKS):
-        for step in range(3):
-            ring(c - 1, step)
-        work(c)
-        ring(c - 1, 3)
-        if c < last:
+        pump()
+        if c >= 1:
+            gather(c - 1)
+        pump(2)
+        spread(c)
+        pump(2)
+        if c >= 1:
             finish(c - 1)
-    ring(last, 0)
+    begin(3)
+    terms(3)
+    gather(2)
+    terms(4)
+    spread(3)
+    raws(3)
+    spread(4)
     answer()
-    finish(last - 1)
-    for step in range(1, 4):
-        ring(last, step)
+    finish(2)
+    gather(3)
+    collect()
+    gather(4)
+    finish(3)
     gate_gradients()
-    finish(last)
-
-    for c in range(CHUNKS):
-        all_pairs(c).wait_send()
+    finish(4)
+
+    for b in range(len(BATCHES) - WINDOW, len(BATCHES)):
+        drain(b)
+    for c in range(len(UNITS)):
         for e in range(2):
             twin_copy(c, e).wait_send()
         for way in range(2):
-            for step in range(4):
-                ring_copy(c, way, step).wait_send()
+            for kind in range(4):
+                hop(c, way, kind).wait_send()
         store_wg(c).wait()
     ret_copies().wait_send()
     store_hg().wait()
 
 
 def body(grad_out, route_ids, route_probs, hidden, w_down):
-    hid = hidden[0].transpose(1, 0, 2, 3).reshape(2, 256, H)
     any_space = pl.BlockSpec(memory_space=pl.ANY)
     vmem = pl.BlockSpec(memory_space=pltpu.VMEM)
     dma = pltpu.SemaphoreType.DMA
     hg, prob, wg = pl.pallas_call(
         kernel,
         out_shape=(
-            jax.ShapeDtypeStruct((2, 256, H), BF16),
+            jax.ShapeDtypeStruct((GROUPS, 2, 4, H), BF16),
             jax.ShapeDtypeStruct((2, TOK), F32),
-            jax.ShapeDtypeStruct((2, PART, D), F32),
+            jax.ShapeDtypeStruct((PART, 2, D), F32),
         ),
         in_specs=[any_space, vmem, vmem, any_space, any_space],
         out_specs=(any_space, vmem, any_space),
         scratch_shapes=[
             pltpu.VMEM((TOK, D), BF16),
             pltpu.VMEM((2, H, D), BF16),
+            pltpu.VMEM((GROUPS, 2, 4, H), BF16),
             pltpu.VMEM((2, 256, H), BF16),
             pltpu.VMEM((2, H, 256), BF16),
             pltpu.VMEM((GROUPS * SLOTS, TOK), BF16),
             pltpu.VMEM((2, 256, max(WIDTHS)), BF16),
             pltpu.VMEM((2, 256, H), F32),
-            pltpu.VMEM((2, 256, H), BF16),
+            pltpu.VMEM((GROUPS, 2, 4, H), BF16),
             pltpu.VMEM((GROUPS, 1, 128), F32),
             pltpu.VMEM((GROUPS, 1, 128), F32),
             pltpu.VMEM((GROUPS, 128), F32),
             [pltpu.VMEM((GROUPS, SLOTS, w), BF16) for w in WIDTHS],
             [pltpu.VMEM((GROUPS, SLOTS, w), BF16) for w in WIDTHS],
-            [pltpu.VMEM((2, SIDE, 2, PART, w), BF16) for w in WIDTHS],
-            [pltpu.VMEM((2, SIDE, PART, w), BF16) for w in WIDTHS],
-            [pltpu.VMEM((2, 4, 2, PART, w), BF16) for w in WIDTHS],
-            [pltpu.VMEM((2, 4, 2, PART, w), BF16) for w in WIDTHS],
-            pltpu.VMEM((2, PART, D), F32),
+            [pltpu.VMEM((2, SIDE, 2, PART, w), BF16) for _, _, w in UNITS],
+            [pltpu.VMEM((2, SIDE, PART, w), BF16) for _, _, w in UNITS],
+            [pltpu.VMEM((2, 4, 2, PART, w), BF16) for _, _, w in UNITS],
+            [pltpu.VMEM((2, 4, 2, PART, w), BF16) for _, _, w in UNITS],
+            pltpu.VMEM((PART, 2, D), F32),
             dma((3,)),
+            dma((len(BATCHES),)),
             dma((CHUNKS,)),
             dma((CHUNKS,)),
-            dma((CHUNKS,)),
-            dma((CHUNKS, 2)),
-            dma((CHUNKS, 2)),
-            dma((CHUNKS, 2, 4)),
-            dma((CHUNKS, 2, 4)),
+            dma((len(UNITS), 2)),
+            dma((len(UNITS), 2)),
+            dma((len(UNITS), 2, 4)),
+            dma((len(UNITS), 2, 4)),
             dma,
             dma,
             dma,
-            dma((CHUNKS + 1,)),
+            dma((len(UNITS) + 1,)),
         ],
         compiler_params=pltpu.CompilerParams(
             collective_id=0, has_side_effects=True, vmem_limit_bytes=56 * 2**20
         ),
         name="routed_backward",
-    )(grad_out, route_ids.T, route_probs.T, hid, w_down)
-    hidden_grad = hg.reshape(2, GROUPS, 4, H).transpose(1, 0, 2, 3)[None]
-    return hidden_grad, prob.T, wg.transpose(1, 0, 2)
+    )(grad_out, route_ids.T, route_probs.T, hidden[0], w_down)
+    return hg[None], prob.T, wg
 
 
 def solution(mesh):

time: 122 us -> 107 us (0.88)
  the two profiles are of different devices: /device:TPU:128 before, /device:TPU:14 now
where the time goes in v2:
time: 107 us; the launch traced here: 106 us
  Pallas kernels  100 us (93%)
  local copies, waits for them, and re-layouts  5.58 us (5%)
    pallas_call x1, Pallas kernels, body(): pl.pallas_call(kernel, out_shape=(jax.ShapeDtypeStruct((GROUPS, 2, 4, H),...  100 us
    unnamed x3, local copies, waits for them, and re-layouts  5.58 us

profile of v2, /device:TPU:14, one launch (start us, length us, event | category | flops | bytes accessed | tf_op | source)
XLA Modules:
  0.0 106.5 jit_solution(5339026560297345170)
XLA Ops:
  0.6 100.2 %routed_backward.1 = (bf16[64,2,4,768]{3,2,1,0:T(4,128)(2,1)}, f32[2,128]{1,0:T(2,128)}, f32[48,2,2048]{2,1,0:T(2,128)}) custom-call(bf16[128,2048]{1,0:T(8,128)(2,1)} %grad_ref.1, s32[2,128]{1,0:T(2,128)} %bitcast.7, f32[2,128]{1,0:T(2,128)} %bitcast.8, bf16[64,2,4,768]{3,2,1,0:T(4,128)(2,1)} %bitcast.5, bf16[2,768,2048]{2,1,0:T(8,128)(2,1)} %w_ref.1), custom_call_target="tpu_custom_call" | custom-call | tf_op jit(solution)/shard_map/routed_backward/pallas_call | solution.py:386
  100.9 2.3 %copy.11 = bf16[1,64,2,4,768]{4,3,2,1,0:T(4,128)(2,1)} copy(bf16[1,64,2,4,768]{4,3,2,1,0:T(4,128)(2,1)} %bitcast.6) | data formatting | bytes 1572864
  103.2 1.2 %copy.12 = f32[128,2]{0,1:T(2,128)} copy(f32[128,2]{0,1:T(2,128)} %bitcast.9) | data formatting | bytes 2048
  104.4 2.1 %copy.13 = f32[48,2,2048]{2,1,0:T(2,128)} copy(f32[48,2,2048]{2,1,0:T(2,128)} %get-tuple-element.14) | data formatting | bytes 1572864

commit v3 on v2

--- a/solution.py
+++ b/solution.py
@@ -8,13 +8,14 @@
 MESH = pl.DeviceIdType.MESH
 F32 = jnp.float32
 BF16 = jnp.bfloat16
-WIDTHS = (512, 512, 512, 512)
+WIDTHS = (512, 512, 512, 384, 128)
 STARTS = tuple(sum(WIDTHS[:i]) for i in range(len(WIDTHS)))
 CHUNKS = len(WIDTHS)
-UNITS = ((0, 0, 512), (1, 0, 512), (2, 0, 512), (3, 0, 256), (3, 256, 256))
+UNITS = ((0, 0, 512), (1, 0, 512), (2, 0, 512), (3, 0, 384), (4, 0, 128))
 WINDOW = 8
-BATCHES = tuple((c, k, k + 4096 // w) for c, w in enumerate(WIDTHS) for k in range(0, 64, 4096 // w))
-ENDS = tuple(sum(w // 64 for w in WIDTHS[: c + 1]) for c in range(len(WIDTHS)))
+PAIRS = tuple(32 if w == 128 else 8 for w in WIDTHS)
+BATCHES = tuple((c, k, k + n) for c, n in enumerate(PAIRS) for k in range(0, 64, n))
+ENDS = tuple(sum(64 // n for n in PAIRS[: c + 1]) for c in range(len(WIDTHS)))
 SIDE = 8
 GROUPS = 64
 SLOTS = 8
@@ -352,14 +353,16 @@
             finish(c - 1)
     begin(3)
     terms(3)
+    raws(3)
     gather(2)
+    spread(3)
+    begin(4)
     terms(4)
-    spread(3)
-    raws(3)
+    raws(4)
     spread(4)
     answer()
+    gather(3)
     finish(2)
-    gather(3)
     collect()
     gather(4)
     finish(3)

time: 107 us -> 106 us (level)
  Pallas kernels: 100 us -> 98.7 us
    pallas_call x1, Pallas kernels: 100 us -> 98.7 us  [body(): pl.pallas_call(kernel, out_shape=(jax.ShapeDtypeStruct((GROUPS, 2, 4, H),...]
where the time goes in v3:
time: 106 us; the launch traced here: 105 us
  Pallas kernels  98.7 us (93%)
  local copies, waits for them, and re-layouts  5.58 us (5%)
    pallas_call x1, Pallas kernels, body(): pl.pallas_call(kernel, out_shape=(jax.ShapeDtypeStruct((GROUPS, 2, 4, H),...  98.7 us
    unnamed x3, local copies, waits for them, and re-layouts  5.58 us

profile of v3, /device:TPU:14, one launch (start us, length us, event | category | flops | bytes accessed | tf_op | source)
XLA Modules:
  0.0 104.9 jit_solution(8510281188431389832)
XLA Ops:
  0.6 98.7 %routed_backward.1 = (bf16[64,2,4,768]{3,2,1,0:T(4,128)(2,1)}, f32[2,128]{1,0:T(2,128)}, f32[48,2,2048]{2,1,0:T(2,128)}) custom-call(bf16[128,2048]{1,0:T(8,128)(2,1)} %grad_ref.1, s32[2,128]{1,0:T(2,128)} %bitcast.7, f32[2,128]{1,0:T(2,128)} %bitcast.8, bf16[64,2,4,768]{3,2,1,0:T(4,128)(2,1)} %bitcast.5, bf16[2,768,2048]{2,1,0:T(8,128)(2,1)} %w_ref.1), custom_call_target="tpu_custom_call" | custom-call | tf_op jit(solution)/shard_map/routed_backward/pallas_call | solution.py:389
  99.3 2.3 %copy.11 = bf16[1,64,2,4,768]{4,3,2,1,0:T(4,128)(2,1)} copy(bf16[1,64,2,4,768]{4,3,2,1,0:T(4,128)(2,1)} %bitcast.6) | data formatting | bytes 1572864
  101.6 1.2 %copy.12 = f32[128,2]{0,1:T(2,128)} copy(f32[128,2]{0,1:T(2,128)} %bitcast.9) | data formatting | bytes 2048
  102.8 2.1 %copy.13 = f32[48,2,2048]{2,1,0:T(2,128)} copy(f32[48,2,2048]{2,1,0:T(2,128)} %get-tuple-element.14) | data formatting | bytes 1572864
